TPU v7x, 32 devices: a whole 2x2x4 slice. The times are simulated.
32 devices in a mesh: seq: 8 (over z, y), batch: 4 (over x, core).
Axes of the slice: x: 2, y: 2, z: 4, core: 2. Of those that a mesh axis runs over, the one named last changes fastest.
Arguments:
- tokens: bfloat16 [4, 3072, 1024], P('batch', 'seq'), may hold values from -6 to 6
- memory: bfloat16 [4, 512, 1024], P('batch', 'seq'), may hold values from -6 to 6
- segment_ids: int32 [4, 3072], P('batch', 'seq'), may hold values from 0 to 2, as said below
- padding_mask: int32 [4, 3072], P('batch', 'seq'), may hold values from 0 to 1, as said below
- cotangent: bfloat16 [4, 3072, 1024], P('batch', 'seq'), may hold values from -6 to 6
- prefix_embed: bfloat16 [30, 1024], replicated, may hold values from -6 to 6
- prefix_first: bfloat16 [1024, 512], replicated, may hold values from -0.1875 to 0.1875
- first_bias: float32 [512], replicated, may hold values from -3 to 3
- prefix_second: bfloat16 [512, 2048], replicated, may hold values from -0.25 to 0.25
- second_bias: float32 [2048], replicated, may hold values from -3 to 3
- adapter_down: bfloat16 [1024, 512], replicated, may hold values from -0.1875 to 0.1875
- down_bias: float32 [512], replicated, may hold values from -3 to 3
- adapter_raise: bfloat16 [512, 1024], replicated, may hold values from -0.0625 to 0.0625
- raise_bias: float32 [1024], replicated, may hold values from -2 to 2
- norm_gain: float32 [3, 1024], replicated, may hold values from 0.25 to 1.75
- norm_shift: float32 [3, 1024], replicated, may hold values from -2 to 2
- self_query: bfloat16 [1024, 1024], replicated, may hold values from -0.1875 to 0.1875
- self_key: bfloat16 [1024, 1024], replicated, may hold values from -0.1875 to 0.1875
- self_value: bfloat16 [1024, 1024], replicated, may hold values from -0.1875 to 0.1875
- self_output: bfloat16 [1024, 1024], replicated, may hold values from -3 to 3
- cross_query: bfloat16 [1024, 1024], replicated, may hold values from -0.1875 to 0.1875
- cross_key: bfloat16 [1024, 1024], replicated, may hold values from -0.1875 to 0.1875
- cross_value: bfloat16 [1024, 1024], replicated, may hold values from -0.1875 to 0.1875
- cross_output: bfloat16 [1024, 1024], replicated, may hold values from -3 to 3
- feed_in: bfloat16 [1024, 4096], replicated, may hold values from -0.1875 to 0.1875
- feed_out: bfloat16 [4096, 1024], replicated, may hold values from -0.09375 to 0.09375
Outputs:
- layer_output: bfloat16 [4, 3072, 1024], P('batch', 'seq')
- token_grad: bfloat16 [4, 3072, 1024], P('batch', 'seq')
- memory_grad: bfloat16 [4, 512, 1024], P('batch', 'seq')
- embed_grad: float32 [30, 1024], replicated
- first_weight_grad: float32 [1024, 512], replicated
- first_bias_grad: float32 [512], replicated
- second_weight_grad: float32 [512, 2048], replicated
- second_bias_grad: float32 [2048], replicated
- down_weight_grad: float32 [1024, 512], replicated
- down_bias_grad: float32 [512], replicated
- raise_weight_grad: float32 [512, 1024], replicated
- raise_bias_grad: float32 [1024], replicated
- gain_grad: float32 [3, 1024], replicated
- shift_grad: float32 [3, 1024], replicated
Inputs may be any that keep to these rules, and one draw needn't show every extreme that they name: `segment_ids`: each row is 0 on its first 1 to 192 positions, then 1 up to a position from 2880 to 2976, then 2 to its end. `padding_mask`: each row is 0 on its last 1 to 96 positions and on one run of 1 to 96 positions that starts between 384 and 2304, and 1 elsewhere.
All inputs are finite; a program needn't handle non-finite values.
Results may differ from a plain program's by a relative error of at most 0.033.
Values may be sent and summed in bfloat16 or wider, within the bound.
A program may use at most 320 MiB of HBM per device.

v0:
```python
import functools

import jax
import jax.numpy as jnp
from jax import lax
from jax.experimental import pallas as pl
from jax.experimental.pallas import tpu as pltpu
from jax.sharding import PartitionSpec as P

H = 16
HD = 64
LANES = 128
PREFIX_ROWS = 32
VMEM_BYTES = 60 * 1024 * 1024
SUM_ROWS = 16
MESH = pl.DeviceIdType.MESH

masked_score = -1e30
norm_eps = 1e-05

def dot_nn(left, right):
    return lax.dot_general(
        left, right, (((1,), (0,)), ((), ())), preferred_element_type=jnp.float32
    )


def dot_nt(left, right):
    return lax.dot_general(
        left, right, (((1,), (1,)), ((), ())), preferred_element_type=jnp.float32
    )


def dot_tn(left, right):
    return lax.dot_general(
        left, right, (((0,), (0,)), ((), ())), preferred_element_type=jnp.float32
    )


def remote(source, target, send_sem, recv_sem, axis, peer):
    return pltpu.make_async_remote_copy(
        src_ref=source,
        dst_ref=target,
        send_sem=send_sem,
        recv_sem=recv_sem,
        device_id={axis: peer},
        device_id_type=MESH,
    )


def enter(sizes):
    barrier = pltpu.get_barrier_semaphore()
    for axis, size in sizes.items():
        for other in range(size):

            @pl.when(other != lax.axis_index(axis))
            def _():
                pl.semaphore_signal(barrier, inc=1, device_id={axis: other}, device_id_type=MESH)

    pl.semaphore_wait(barrier, sum(sizes.values()) - len(sizes))


def others(size, mine, body):
    for other in range(size):

        @pl.when(other != mine)
        def _():
            body(other)


def rows_of(index, size):
    return pl.ds(pl.multiple_of(index * size, size), size)


def span_of(start, size):
    return pl.ds(pl.multiple_of(start, LANES), size)


def own_columns(ref, first, me, width):
    if width % LANES == 0:
        return ref[:, pl.ds(pl.multiple_of(first + me * width, LANES), width)].astype(jnp.float32)
    share = LANES // width
    block = ref[:, pl.ds(pl.multiple_of(first + me // share * LANES, LANES), LANES)].astype(
        jnp.float32
    )
    picked = block[:, :width]
    for part in range(1, share):
        picked = jnp.where(me % share == part, block[:, part * width : (part + 1) * width], picked)
    return picked


def head_lanes(shape, head):
    lane = lax.broadcasted_iota(jnp.int32, shape, 1)
    return (lane >= head * HD) & (lane < (head + 1) * HD)


def self_forward_kernel(
    n,
    seg_ref,
    pad_ref,
    tok_ref,
    wq_in,
    wk_in,
    wv_in,
    emb_ref,
    first_in,
    fbias_ref,
    second_in,
    sbias_ref,
    mem_ref,
    wck_in,
    wcv_in,
    att_ref,
    mkey_out,
    mvalue_out,
    qx_out,
    kx_out,
    raw_out,
    pk_out,
    pv_out,
    pkt_out,
    ot_out,
    lse_out,
    send,
    recv,
    meta_send,
    meta,
    kx,
    qx,
    vt,
    hidden,
    pk,
    pv,
    pkt,
    pvt,
    stat,
    acc,
    o_send,
    o_recv,
    mem_all,
    wck,
    wcv,
    mkey_ref,
    mvalue_ref,
    wq_ref,
    wk_ref,
    wv_ref,
    first_ref,
    second_ref,
    send_sem,
    recv_sem,
    meta_send_sem,
    meta_recv_sem,
    o_send_sem,
    o_recv_sem,
    mem_send_sem,
    mem_recv_sem,
    out_sem,
    weight_sem,
    in_sem,
):
    low = jnp.bfloat16
    f32 = jnp.float32
    me = lax.axis_index("seq")
    length, width = tok_ref.shape
    group = width // n
    heads = group // HD
    plane = 2 * length
    planes = n // 2
    block = 2 * LANES
    per_block = block // group
    blocks = width // block
    my_plane = me // 2
    my_side = lax.rem(me, 2)

    upward = my_plane >= planes // 2
    turn_sign = jnp.where(upward, 1, -1)

    def plane_after(step):
        return lax.rem(my_plane + planes + turn_sign * step, planes)

    def meta_copy(peer, slot):
        return remote(
            meta_send, meta.at[slot], meta_send_sem.at[peer], meta_recv_sem.at[slot], "seq", peer
        )

    def qkv_copy(head, peer, slot):
        return remote(
            send.at[peer, head],
            recv.at[head, slot],
            send_sem.at[head, peer],
            recv_sem.at[head, slot],
            "seq",
            peer,
        )

    def out_copy(head, peer, slot):
        return remote(
            o_send.at[head, peer],
            o_recv.at[slot, head],
            o_send_sem.at[head, peer],
            o_recv_sem.at[head, slot],
            "seq",
            peer,
        )

    def mem_along(which, toward):
        part = mem_all.at[which, my_side]
        return remote(
            part,
            part,
            mem_send_sem.at[(toward + 1) // 2, which],
            mem_recv_sem.at[which],
            "seq",
            me + 2 * toward,
        )

    def mem_across(side):
        part = mem_all.at[:, side]
        return remote(
            part,
            part,
            mem_send_sem.at[0, planes],
            mem_recv_sem.at[planes],
            "seq",
            me + 1 - 2 * my_side,
        )

    def mem_hops(hop, body):
        for toward in (1, -1):
            which = my_plane - toward * hop
            ahead = my_plane + toward

            @pl.when((which >= 0) & (which < planes) & (ahead >= 0) & (ahead < planes))
            def _():
                body(mem_along(which, toward))

    def mem_arrivals(hop):
        for toward in (1, -1):
            which = my_plane - toward * hop

            @pl.when((which >= 0) & (which < planes))
            def _():
                mem_along(which, -toward).wait_recv()

    def block_at(step):
        if blocks >= planes:
            share = blocks // planes
            return plane_after(1 + step // share) * share + step % share
        return lax.rem(me // per_block + 1 + step, blocks)

    def weight_load(step, which):
        columns = rows_of(block_at(step), block)
        source = (wq_in, wk_in, wv_in)[which]
        target = (wq_ref, wk_ref, wv_ref)[which]
        return pltpu.make_async_copy(
            source.at[:, columns], target.at[:, columns], weight_sem.at[step, which]
        )

    for step in range(blocks):
        for which in range(3):
            weight_load(step, which).start()
    loads = [
        pltpu.make_async_copy(source, target, in_sem.at[index])
        for index, (source, target) in enumerate(
            ((first_in, first_ref), (second_in, second_ref), (wck_in, wck), (wcv_in, wcv))
        )
    ]
    for load in loads:
        load.start()
    segments = seg_ref[...]
    tags = jnp.where(pad_ref[...] == 1, segments, -1)
    row = lax.broadcasted_iota(jnp.int32, meta_send.shape, 0)
    meta_send[...] = jnp.where(row == 0, segments, tags)
    mem_all[my_plane, my_side] = mem_ref[...]
    enter({"seq": n})
    others(n, me, lambda peer: meta_copy(peer, me).start())
    meta[me] = meta_send[...]

    for step in range(blocks):
        at = block_at(step)
        columns = rows_of(at, block)
        for which, weight in enumerate((wq_ref, wk_ref, wv_ref)):
            weight_load(step, which).wait()
            piece = dot_nn(tok_ref[...], weight[:, columns]).T.astype(low)
            for part in range(per_block):
                for head in range(heads):
                    first = part * group + head * HD
                    send[at * per_block + part, head, which] = piece[first : first + HD]
        for part in range(per_block):
            peer = at * per_block + part

            @pl.when(peer != me)
            def _():
                qkv_copy(0, peer, me).start()

            @pl.when(peer == me)
            def _():
                for head in range(heads):
                    recv[head, me] = send[peer, head]

    mem_hops(0, lambda copy: copy.start())
    loads[0].wait()
    loads[1].wait()
    hidden[...] = jnp.zeros_like(hidden)
    hidden[: emb_ref.shape[0], :] = jnp.tanh(dot_nn(emb_ref[...], first_ref[...]) + fbias_ref[...])
    hidden_low = hidden[...].astype(low)
    prefix_key = dot_nn(hidden_low, own_columns(second_ref, 0, me, group).astype(low)) + own_columns(
        sbias_ref, 0, me, group
    )
    prefix_value = dot_nn(
        hidden_low, own_columns(second_ref, width, me, group).astype(low)
    ) + own_columns(sbias_ref, width, me, group)
    prefix_row = lax.broadcasted_iota(jnp.int32, (PREFIX_ROWS, HD), 0)
    prefix_open = jnp.where(prefix_row < emb_ref.shape[0], 0.0, masked_score)
    for head in range(heads):
        here = slice(head * HD, (head + 1) * HD)
        pk[head] = jnp.concatenate([prefix_key[:, here], prefix_open], axis=1).astype(low)
        pv[head] = prefix_value[:, here].astype(low)
    pkt[...] = prefix_key.T.astype(low).reshape(heads, HD, PREFIX_ROWS)
    pvt[:, :HD, :] = prefix_value.T.astype(low).reshape(heads, HD, PREFIX_ROWS)
    pvt[:, HD:, :] = jnp.ones((heads, SUM_ROWS, PREFIX_ROWS), low)
    vt[:, HD:, :] = jnp.ones((heads, SUM_ROWS, n * length), low)

    def arrive(head, chunk):
        @pl.when(chunk != me)
        def _():
            @pl.when(head == 0)
            def _():
                meta_copy(chunk, chunk).wait_recv()

            qkv_copy(head, chunk, chunk).wait_recv()

        here = rows_of(chunk, length)
        state = lax.broadcasted_iota(jnp.int32, (HD, length), 0)
        qx[head, :HD, here] = (recv[head, chunk, 0].astype(f32) * 0.125).astype(low)
        qx[head, HD:, here] = jnp.where(state == meta[chunk, 0:1, :], 1.0, 0.0).astype(low)
        is_open = jnp.where(state == meta[chunk, 1:2, :], 0.0, masked_score)
        kx[head, here, :] = jnp.concatenate(
            [recv[head, chunk, 1].astype(f32), is_open], axis=0
        ).T.astype(low)
        vt[head, :HD, here] = recv[head, chunk, 2]

    def open_plane(head, which):
        scores = dot_nn(pk[head], qx[head, :, rows_of(which, plane)])
        top = jnp.max(scores, axis=0, keepdims=True)
        raised = jnp.exp(scores - top)
        stat[which, head, 0:1, :] = top
        acc[which, head] = dot_nn(pvt[head], raised.astype(low))

    def pair_part(head, upper, lower, first, count, keys, diagonal):
        here = slice(first, first + count)
        queries = qx[head, :, span_of(upper * plane + first, count)]
        key_rows = span_of(lower * plane, keys)
        scores = dot_nn(kx[head, key_rows, :], queries)
        if diagonal:
            key_at = lax.broadcasted_iota(jnp.int32, scores.shape, 0)
            query_at = lax.broadcasted_iota(jnp.int32, scores.shape, 1) + first
            scores = jnp.where(key_at <= query_at, scores, masked_score)
        old_top = stat[upper, head, 0:1, here]
        top = jnp.maximum(old_top, jnp.max(scores, axis=0, keepdims=True))
        raised = jnp.exp(scores - top).astype(low)
        stat[upper, head, 0:1, here] = top
        acc[upper, head, :, here] = acc[upper, head, :, here] * jnp.exp(old_top - top) + dot_nn(
            vt[head, :, key_rows], raised
        )

    def pair(head, upper, lower):
        pair_part(head, upper, lower, 0, plane, plane, False)

    def pair_diagonal(head, which):
        for part in range(2):
            pair_part(head, which, which, part * length, length, (part + 1) * length, True)

    def close_plane(head, which):
        total = acc[which, head, HD : HD + 1, :]
        value = acc[which, head, :HD, :] / total
        acc[which, head, :HD, :] = value
        stat[which, head, 0:1, :] = stat[which, head, 0:1, :] + jnp.log(total)
        for part in range(2):
            chunk = 2 * which + part
            o_send[head, chunk] = value[:, part * length : (part + 1) * length].astype(low)

            @pl.when((chunk != me) & (head == heads - 1))
            def _():
                out_copy(head, chunk, me).start()

            @pl.when(chunk == me)
            def _():
                o_recv[me, head] = o_send[head, chunk]

    def project_memory():
        mem_across(1 - my_side).wait_recv()
        for load in loads[2:]:
            load.wait()
        whole = mem_all[...].reshape(mkey_ref.shape)

        def one(index, carry):
            here = rows_of(index, block)
            mkey_ref[:, here] = dot_nn(whole, wck[:, here]).astype(low)
            mvalue_ref[:, here] = dot_nn(whole, wcv[:, here]).astype(low)
            return carry

        lax.fori_loop(0, blocks, one, 0)

    def stage(index, carry):
        head = index // planes
        step = lax.rem(index, planes)

        @pl.when(head + 1 < heads)
        def _():
            there = plane_after(1 + step)
            for part in range(2):
                peer = 2 * there + part

                @pl.when(peer != me)
                def _():
                    qkv_copy(head, peer, me).wait_send()
                    qkv_copy(head + 1, peer, me).start()

        @pl.when((head == heads - 1) & (head > 0))
        def _():
            there = plane_after(1 + step)
            for part in range(2):
                peer = 2 * there + part

                @pl.when(peer != me)
                def _():
                    qkv_copy(head, peer, me).wait_send()
                    out_copy(head - 1, peer, me).start()

        here = plane_after(step)
        arrive(head, 2 * here)
        arrive(head, 2 * here + 1)
        open_plane(head, here)
        pair_diagonal(head, here)

        def earlier(back, inner):
            there = plane_after(back)
            pair(head, jnp.maximum(here, there), jnp.minimum(here, there))

            @pl.when((step == planes - 1) & (there > here))
            def _():
                close_plane(head, there)

            return inner

        lax.fori_loop(0, step, earlier, 0)
        for hop in range(1, planes - 1):

            @pl.when(index == hop)
            def _():
                mem_arrivals(hop)
                mem_hops(hop, lambda copy: copy.start())

        @pl.when(index == planes - 1)
        def _():
            mem_arrivals(planes - 1)
            mem_across(my_side).start()

        @pl.when((upward & (my_plane + step >= planes)) | (step == planes - 1))
        def _():
            close_plane(head, here)

        @pl.when(jnp.logical_not(upward) & (step == my_plane))
        def _():
            def close(which, inner):
                close_plane(head, which)
                return inner

            lax.fori_loop(0, my_plane + 1, close, 0)

        return carry

    lax.fori_loop(0, heads * planes, stage, 0)

    saves = []

    def save(source, target):
        copy = pltpu.make_async_copy(source, target, out_sem.at[len(saves)])
        copy.start()
        saves.append(copy)

    save(qx, qx_out)
    save(kx, kx_out)
    save(recv, raw_out)
    save(pk, pk_out)
    save(pv, pv_out)
    save(pkt, pkt_out)
    save(acc, ot_out)
    save(stat, lse_out)
    project_memory()
    save(mkey_ref, mkey_out)
    save(mvalue_ref, mvalue_out)
    for other in range(n):

        @pl.when(other != me)
        def _():
            for head in range(heads):
                out_copy(head, other, other).wait_recv()

        att_ref[:, other * group : (other + 1) * group] = (
            o_recv[other].reshape(group, length).astype(f32).T.astype(low)
        )

    def drain(peer):
        meta_copy(peer, me).wait_send()
        if heads == 1:
            qkv_copy(0, peer, me).wait_send()
        for head in range(heads):
            out_copy(head, peer, me).wait_send()

    others(n, me, drain)
    for hop in range(planes - 1):
        mem_hops(hop, lambda copy: copy.wait_send())
    mem_across(my_side).wait_send()
    for copy in saves:
        copy.wait()


def self_forward(n, segments, padding, tokens, weights, prefix, memory, mem_weights):
    length, width = tokens.shape
    group = width // n
    heads = group // HD
    whole = n * length
    planes = n // 2
    low = jnp.bfloat16
    f32 = jnp.float32
    vmem = pl.BlockSpec(memory_space=pltpu.VMEM)
    anywhere = pl.BlockSpec(memory_space=pl.ANY)
    dma = pltpu.SemaphoreType.DMA
    shapes = (
        ((heads, 2 * HD, whole), low),
        ((heads, whole, 2 * HD), low),
        ((heads, n, 3, HD, length), low),
        ((heads, PREFIX_ROWS, 2 * HD), low),
        ((heads, PREFIX_ROWS, HD), low),
        ((heads, HD, PREFIX_ROWS), low),
        ((planes, heads, HD + SUM_ROWS, 2 * length), f32),
        ((planes, heads, 8, 2 * length), f32),
    )
    square = pltpu.VMEM((width, width), low)
    qx, kx, raw, pk, pv, pkt, acc, stat = (pltpu.VMEM(*shape) for shape in shapes)
    return pl.pallas_call(
        functools.partial(self_forward_kernel, n),
        out_shape=(
            jax.ShapeDtypeStruct((length, width), low),
            jax.ShapeDtypeStruct((n * memory.shape[0], width), low),
            jax.ShapeDtypeStruct((n * memory.shape[0], width), low),
        )
        + tuple(jax.ShapeDtypeStruct(*shape) for shape in shapes),
        in_specs=[vmem] * 3
        + [anywhere] * 3
        + [vmem, anywhere, vmem, anywhere, vmem, vmem]
        + [anywhere] * 2,
        out_specs=(vmem,) + (anywhere,) * 10,
        scratch_shapes=[
            pltpu.VMEM((n, heads, 3, HD, length), low),
            raw,
            pltpu.VMEM((8, length), jnp.int32),
            pltpu.VMEM((n, 8, length), jnp.int32),
            kx,
            qx,
            pltpu.VMEM((heads, HD + SUM_ROWS, whole), low),
            pltpu.VMEM((PREFIX_ROWS, weights[0].shape[0] // 2), f32),
            pk,
            pv,
            pkt,
            pltpu.VMEM((heads, HD + SUM_ROWS, PREFIX_ROWS), low),
            stat,
            acc,
            pltpu.VMEM((heads, n, HD, length), low),
            pltpu.VMEM((n, heads, HD, length), low),
            pltpu.VMEM((planes, 2) + memory.shape, low),
            square,
            square,
            pltpu.VMEM((n * memory.shape[0], width), low),
            pltpu.VMEM((n * memory.shape[0], width), low),
            square,
            square,
            square,
            pltpu.VMEM(prefix[1].shape, low),
            pltpu.VMEM(prefix[3].shape, low),
            dma((heads, n)),
            dma((heads, n)),
            dma((n,)),
            dma((n,)),
            dma((heads, n)),
            dma((heads, n)),
            dma((2, planes + 1)),
            dma((planes + 1,)),
            dma((10,)),
            dma((width // (2 * LANES), 3)),
            dma((4,)),
        ],
        compiler_params=pltpu.CompilerParams(
            collective_id=0, has_side_effects=True, vmem_limit_bytes=VMEM_BYTES
        ),
        name="self_forward",
    )(segments, padding, tokens, *weights, *prefix, memory, *mem_weights)


def self_backward_kernel(
    n,
    batches,
    base_in,
    do_in,
    sums_in,
    mkey_in,
    mvalue_in,
    wck_in,
    wcv_in,
    vecs_in,
    qx_in,
    kx_in,
    raw_in,
    pk_in,
    pv_in,
    pkt_in,
    ot_in,
    lse_in,
    wq_in,
    wk_in,
    wv_in,
    tg_ref,
    mgrad_ref,
    pkv_ref,
    vecs_ref,
    full_out,
    do_recv,
    qx,
    kx,
    raw,
    kt,
    values,
    dot,
    qdo,
    pk,
    pv,
    pkt,
    ot,
    stat,
    weights,
    dqt,
    dkv,
    g_send,
    g_recv,
    pre_ref,
    pre_all,
    pre_sum,
    pre_recv,
    sums_mine,
    sums_core,
    sums_x,
    sums_side,
    sums_z,
    full,
    mkey,
    mvalue,
    wck,
    wcv,
    mem_part,
    mem_side,
    mem_up,
    mem_down,
    vec_all,
    vec_sum,
    vec_y,
    vec_both,
    vec_z,
    product,
    base_ref,
    do_send_sem,
    do_recv_sem,
    g_send_sem,
    g_recv_sem,
    in_sem,
    send_sem,
    recv_sem,
):
    low = jnp.bfloat16
    f32 = jnp.float32
    me = lax.axis_index("seq")
    length, width = tg_ref.shape
    group = width // n
    heads = group // HD
    plane = 2 * length
    planes = n // 2
    step_rows = 256
    my_batch = lax.axis_index("batch")
    my_core = lax.rem(my_batch, 2)
    my_high = my_batch // 2
    highs = batches // 2
    my_plane = me // 2
    my_side = lax.rem(me, 2)
    beside = me + 1 - 2 * my_side
    used = [0]

    def numbers(count):
        used[0] += count
        return used[0] - count

    core_slot = numbers(2)
    x_slot = numbers(2 * highs)
    y_slot = numbers(3)
    z_slot = numbers(2 * planes)
    up_slot = numbers(planes)
    down_slot = numbers(planes)
    va_slot = numbers(batches)
    vb_slot = numbers(1)
    vc_slot = numbers(planes)
    pa_slot = numbers(batches)
    pb_slot = numbers(n)

    def send(source, target, first, peer_index, slot_index, axis, peer):
        return remote(
            source,
            target,
            send_sem.at[first + peer_index],
            recv_sem.at[first + slot_index],
            axis,
            peer,
        )

    half_rows = 2 * planes * highs * sums_z.shape[1]
    x_rows = half_rows // highs
    y_rows = x_rows // 2
    z_rows = y_rows // planes
    x_row = pl.multiple_of(my_high * x_rows, x_rows)
    y_row = pl.multiple_of(x_row + my_side * y_rows, y_rows)

    def part(row, count):
        return sums_mine.at[pl.ds(pl.multiple_of(row, count), count)]

    def reduce_core():
        return send(
            sums_in.at[1 - my_core], sums_core, core_slot, 0, 0, "batch", my_batch + 1 - 2 * my_core
        )

    def reduce_x(peer, slot):
        return send(
            part(peer * x_rows, x_rows),
            sums_x.at[slot],
            x_slot,
            peer,
            slot,
            "batch",
            2 * peer + my_core,
        )

    def reduce_y():
        return send(
            part(x_row + (1 - my_side) * y_rows, y_rows), sums_side, y_slot, 0, 0, "seq", beside
        )

    def reduce_z(peer, slot):
        return send(
            part(y_row + peer * z_rows, z_rows),
            sums_z.at[slot],
            z_slot,
            peer,
            slot,
            "seq",
            2 * peer + my_side,
        )

    def gather_z(peer, slot):
        piece = full.at[my_core, my_high, my_side, slot]
        return send(piece, piece, z_slot + planes, peer, slot, "seq", 2 * peer + my_side)

    def gather_y(side):
        piece = full.at[my_core, my_high, side]
        return send(piece, piece, y_slot + 1, 0, 0, "seq", beside)

    def gather_x(peer, slot):
        piece = full.at[my_core, slot]
        return send(piece, piece, x_slot + highs, peer, slot, "batch", 2 * peer + my_core)

    def gather_core(core):
        piece = full.at[core]
        return send(piece, piece, core_slot + 1, 0, 0, "batch", my_batch + 1 - 2 * my_core)

    def mem_across():
        return send(
            mem_part.at[:, 1 - my_side], mem_side, y_slot + 2, 0, 0, "seq", beside
        )

    def mem_hop(target, toward, peer=None):
        buffer, slot = (mem_up, up_slot) if toward > 0 else (mem_down, down_slot)
        return send(
            mem_part.at[target, my_side],
            buffer.at[target],
            slot,
            target,
            target,
            "seq",
            me + 2 * toward if peer is None else peer,
        )

    def mem_from(target, toward):
        return mem_hop(target, toward, me - 2 * toward)

    def mem_pass(toward):
        buffer = mem_up if toward > 0 else mem_down
        first = 0 if toward > 0 else planes - 1
        for target in range(planes):

            @pl.when((target - my_plane) * toward > 0)
            def _():
                @pl.when(my_plane != first)
                def _():
                    mem_from(target, toward).wait_recv()
                    mem_part[target, my_side] = (
                        mem_part[target, my_side].astype(f32) + buffer[target].astype(f32)
                    ).astype(low)

                mem_hop(target, toward).start()

    def mem_stage(at):
        pl.when(my_plane == at)(lambda: mem_pass(1))
        pl.when(my_plane == planes - 1 - at)(lambda: mem_pass(-1))

    def mem_end():
        value = mem_part[my_plane, my_side].astype(f32)
        mgrad_ref[...] = value.astype(low)

        @pl.when(my_plane > 0)
        def _():
            mem_from(my_plane, 1).wait_recv()
            mgrad_ref[...] = (mgrad_ref[...].astype(f32) + mem_up[my_plane].astype(f32)).astype(low)

        @pl.when(my_plane < planes - 1)
        def _():
            mem_from(my_plane, -1).wait_recv()
            mgrad_ref[...] = (
                mgrad_ref[...].astype(f32) + mem_down[my_plane].astype(f32)
            ).astype(low)

    def mem_drain():
        for target in range(planes):

            @pl.when(target > my_plane)
            def _():
                mem_hop(target, 1).wait_send()

            @pl.when(target < my_plane)
            def _():
                mem_hop(target, -1).wait_send()

    def vec_a(peer, slot):
        return send(vecs_in, vec_all.at[slot], va_slot, peer, slot, "batch", peer)

    def vec_b(side):
        return send(vec_sum, vec_y.at[side], vb_slot, 0, 0, "seq", beside)

    def vec_c(peer, slot):
        return send(vec_both, vec_z.at[slot], vc_slot, peer, slot, "seq", 2 * peer + my_side)

    def pre_a(peer, slot):
        return send(pre_ref, pre_all.at[slot], pa_slot, peer, slot, "batch", peer)

    def pre_b(peer, slot):
        return send(pre_sum, pre_recv.at[slot], pb_slot, peer, slot, "seq", peer)

    def do_copy(head, peer, slot):
        return remote(
            do_in.at[peer, head],
            do_recv.at[head, slot],
            do_send_sem.at[head, peer],
            do_recv_sem.at[head, slot],
            "seq",
            peer,
        )

    def q_copy(head, peer, slot):
        return remote(
            g_send.at[peer, head, 0],
            g_recv.at[0, slot, head],
            g_send_sem.at[0, head, peer],
            g_recv_sem.at[0, head, slot],
            "seq",
            peer,
        )

    def kv_copy(head, peer, slot):
        return remote(
            g_send.at[peer, head, pl.ds(1, 2)],
            g_recv.at[pl.ds(1, 2), slot, head],
            g_send_sem.at[1, head, peer],
            g_recv_sem.at[1, head, slot],
            "seq",
            peer,
        )

    def far_first(body):
        for index in range(n):
            peer = jnp.where(my_plane < planes // 2, n - 1 - index, index)

            @pl.when(peer != me)
            def _():
                body(peer)

    def added(ref, size):
        value = ref[0].astype(f32)
        for other in range(1, size):
            value = value + ref[other].astype(f32)
        return value

    loads = [
        pltpu.make_async_copy(source, target, in_sem.at[index])
        for index, (source, target) in enumerate(
            (
                (raw_in, raw),
                (kx_in, kx),
                (pk_in, pk),
                (pv_in, pv),
                (pkt_in, pkt),
                (qx_in, qx),
                (ot_in, ot),
                (lse_in, stat),
                (sums_in.at[my_core], sums_mine),
                (vecs_in, vec_all.at[my_batch]),
                (mkey_in, mkey),
                (mvalue_in, mvalue),
                (wck_in, wck),
                (wcv_in, wcv),
                (base_in, base_ref),
                (wq_in, weights.at[0]),
                (wk_in, weights.at[1]),
                (wv_in, weights.at[2]),
            )
        )
    ]
    own_do = pltpu.make_async_copy(do_in.at[me], do_recv.at[:, me], in_sem.at[len(loads)])
    own_do.start()
    for load in loads:
        load.start()
    enter({"seq": n, "batch": batches})
    far_first(lambda peer: do_copy(0, peer, me).start())
    reduce_core().start()
    others(batches, my_batch, lambda peer: vec_a(peer, my_batch).start())
    dkv[...] = jnp.zeros_like(dkv)
    product[...] = jnp.zeros_like(product)
    pre_ref[...] = jnp.zeros_like(pre_ref)
    for load in loads[:14]:
        load.wait()
    own_do.wait()

    def turn(index, carry):
        head = index // n
        chunk = lax.rem(index, n)
        here = rows_of(chunk, length)
        kt[head, :, here] = raw[head, chunk, 1]
        values[head, here, :] = raw[head, chunk, 2].astype(f32).T.astype(low)
        return carry

    lax.fori_loop(0, heads * n, turn, 0)

    def memory_back(index, carry):
        here = rows_of(index, step_rows)
        value = dot_nt(mkey[...], wck[here, :]) + dot_nt(mvalue[...], wcv[here, :])
        mem_part[:, :, :, here] = value.astype(low).reshape(mem_part.shape[:3] + (step_rows,))
        return carry

    lax.fori_loop(0, width // step_rows, memory_back, 0)
    mem_across().start()

    def next_head(head):
        def move(peer):
            do_copy(head, peer, me).wait_send()
            do_copy(head + 1, peer, me).start()

        far_first(move)

    def arrive(head, which):
        for part in range(2):
            chunk = 2 * which + part

            @pl.when(chunk != me)
            def _():
                do_copy(head, chunk, chunk).wait_recv()

            grads = do_recv[head, chunk]
            dot[head, :, rows_of(chunk, length)] = grads
            grads = grads.astype(f32)
            query = raw[head, chunk, 0].astype(f32) * 0.125
            qdo[head, rows_of(chunk, length), :] = (
                jnp.concatenate([query, grads], axis=0).T.astype(low)
            )
            here = slice(part * length, (part + 1) * length)
            stat[which, head, 1:2, here] = jnp.sum(
                grads * ot[which, head, :HD, here], axis=0, keepdims=True
            )
        here = rows_of(which, plane)
        weight = jnp.exp(dot_nn(pk[head], qx[head, :, here]) - stat[which, head, 0:1, :])
        slope = weight * (dot_nn(pv[head], dot[head, :, here]) - stat[which, head, 1:2, :])
        both = jnp.concatenate([slope, weight], axis=0).astype(low)
        sums = dot_nn(both, qdo[head, here, :])
        pre_ref[head] += jnp.where(
            head_lanes((PREFIX_ROWS, 2 * HD), 0), sums[:PREFIX_ROWS], sums[PREFIX_ROWS:]
        )
        slope = slope.astype(low)
        dqt[which, head] = dot_nn(pkt[head], slope)

    def plus(first, second):
        return (first.astype(f32) + second.astype(f32)).astype(low)

    def sum_one():
        reduce_core().wait_recv()
        sums_mine[...] = plus(sums_mine[...], sums_core[...])
        others(highs, my_high, lambda peer: reduce_x(peer, my_high).start())

    def sum_two():
        here = pl.ds(x_row, x_rows)
        others(highs, my_high, lambda peer: reduce_x(peer, peer).wait_recv())
        sums_x[my_high] = sums_mine[here]
        sums_mine[here] = added(sums_x, highs).astype(low)
        reduce_y().start()

    def sum_three():
        here = pl.ds(y_row, y_rows)
        reduce_y().wait_recv()
        sums_mine[here] = plus(sums_mine[here], sums_side[...])
        others(planes, my_plane, lambda peer: reduce_z(peer, my_plane).start())

    def sum_four():
        here = pl.ds(pl.multiple_of(y_row + my_plane * z_rows, z_rows), z_rows)
        others(planes, my_plane, lambda peer: reduce_z(peer, peer).wait_recv())
        sums_z[my_plane] = sums_mine[here]
        full[my_core, my_high, my_side, my_plane] = added(sums_z, planes).astype(low)
        others(planes, my_plane, lambda peer: gather_z(peer, my_plane).start())

    def sum_five():
        others(planes, my_plane, lambda peer: gather_z(peer, peer).wait_recv())
        gather_y(my_side).start()

    def sum_six():
        gather_y(1 - my_side).wait_recv()
        others(highs, my_high, lambda peer: gather_x(peer, my_high).start())

    def sum_seven():
        others(highs, my_high, lambda peer: gather_x(peer, peer).wait_recv())
        gather_core(my_core).start()

    def sum_end():
        gather_core(1 - my_core).wait_recv()
        save_full.start()

    def vec_one():
        others(batches, my_batch, lambda peer: vec_a(peer, peer).wait_recv())
        vec_sum[...] = added(vec_all, batches)
        vec_b(my_side).start()
        vec_y[my_side] = vec_sum[...]

    def vec_two():
        vec_b(1 - my_side).wait_recv()
        value = (vec_y[0] + vec_y[1]).astype(f32)
        vec_both[...] = jnp.concatenate(
            [value[:, : width // 2], value[:, width // 2 :]], axis=0
        ).astype(low)
        others(planes, my_plane, lambda peer: vec_c(peer, my_plane).start())
        vec_z[my_plane] = vec_both[...]

    def vec_end():
        others(planes, my_plane, lambda peer: vec_c(peer, peer).wait_recv())
        value = added(vec_z, planes)
        vecs_ref[:, : width // 2] = value[:8]
        vecs_ref[:, width // 2 :] = value[8:]

    def mem_one():
        mem_across().wait_recv()
        mem_part[:, my_side] = plus(mem_part[:, my_side], mem_side[...])

    def stage_pa():
        others(batches, my_batch, lambda peer: pre_a(peer, my_batch).start())
        pre_all[my_batch] = pre_ref[...]

    def stage_pb():
        others(batches, my_batch, lambda peer: pre_a(peer, peer).wait_recv())
        pre_sum[...] = added(pre_all, batches).astype(low)
        others(n, me, lambda peer: pre_b(peer, me).start())
        pre_recv[me] = pre_sum[...]

    save_full = pltpu.make_async_copy(full, full_out, in_sem.at[0])

    def pair_part(head, upper, lower, first, count, diagonal):
        keys = span_of(lower * plane + first, count)
        here = span_of(upper * plane + first, plane - first)
        at = slice(first, plane)
        scores = dot_nn(kx[head, keys, :], qx[head, :, here])
        slope = dot_nn(values[head, keys, :], dot[head, :, here]) - stat[upper, head, 1:2, at]
        weight = jnp.exp(scores - stat[upper, head, 0:1, at])
        if diagonal:
            key_at = lax.broadcasted_iota(jnp.int32, scores.shape, 0)
            query_at = lax.broadcasted_iota(jnp.int32, scores.shape, 1)
            weight = jnp.where(key_at <= query_at, weight, 0.0)
        slope = (weight * slope).astype(low)
        key_part = dot_nn(slope, qdo[head, here, :])
        value_part = dot_nn(weight.astype(low), qdo[head, here, :])
        dkv[head, keys, :] += jnp.where(head_lanes((count, 2 * HD), 0), key_part, value_part)
        dqt[upper, head, :, at] += dot_nn(kt[head, :, keys], slope)

    def pair(head, upper, lower, diagonal):
        if diagonal:
            pair_part(head, upper, lower, 0, length, True)
            pair_part(head, upper, lower, length, length, True)
        else:
            pair_part(head, upper, lower, 0, plane, False)

    def hand_queries(head, which):
        for part in range(2):
            chunk = 2 * which + part
            g_send[chunk, head, 0] = (
                dqt[which, head, :, part * length : (part + 1) * length] * 0.125
            ).astype(low)

            @pl.when(chunk != me)
            def _():
                q_copy(head, chunk, me).start()

            @pl.when(chunk == me)
            def _():
                g_recv[0, me, head] = g_send[chunk, head, 0]

    def hand_keys(head, which):
        for part in range(2):
            chunk = 2 * which + part
            turned = dkv[head, rows_of(chunk, length), :].T.astype(low)
            g_send[chunk, head, 1] = turned[:HD]
            g_send[chunk, head, 2] = turned[HD:]

            @pl.when(chunk != me)
            def _():
                kv_copy(head, chunk, me).start()

            @pl.when(chunk == me)
            def _():
                g_recv[pl.ds(1, 2), me, head] = g_send[chunk, head, pl.ds(1, 2)]

    rising = my_plane >= planes // 2
    total = heads * planes * (planes + 1) // 2
    hooks = [
        (2, sum_one),
        (3, mem_one),
        (4, lambda: mem_stage(0)),
        (5, vec_one),
        (5, sum_two),
        (7, sum_three),
        (8, vec_two),
        (10, sum_four),
        (12, sum_five),
        (14, sum_six),
        (16, vec_end),
        (17, sum_seven),
    ] + [(4 + 3 * at, functools.partial(mem_stage, at)) for at in range(1, planes - 1)]
    hooks += [
        (1 + head * total // heads, functools.partial(next_head, head)) for head in range(heads - 1)
    ]
    final = total - planes * (planes + 1) // 2
    hooks += [(final + planes + 1, stage_pa), (final + 2 * planes - 1, stage_pb)]

    def hook(pairs):
        for number, body in sorted(hooks, key=lambda item: item[0]):
            pl.when(pairs == number)(body)


    def stage(index, carry):
        head = index // planes
        step = lax.rem(index, planes)
        here = jnp.where(rising, step, planes - 1 - step)

        @pl.when((step == 0) | ((step == 1) & jnp.logical_not(rising)))
        def _():
            @pl.when(rising | (step == 0))
            def _():
                arrive(head, here)

            @pl.when(jnp.logical_not(rising) & (step == 1))
            def _():
                def rest(which, inner):
                    arrive(head, planes - 2 - which)
                    return inner

                lax.fori_loop(0, planes - 1, rest, 0)

        begun = head * (planes * (planes + 1) // 2) + step * planes - step * (step - 1) // 2
        hook(begun)
        pair(head, here, here, True)

        @pl.when(rising)
        def _():
            hand_queries(head, here)

        @pl.when(jnp.logical_not(rising))
        def _():
            hand_keys(head, here)

        def far(at, inner):
            there = jnp.where(rising, here + 1 + at, here - 1 - at)

            @pl.when(rising & (step == 0))
            def _():
                arrive(head, there)

            hook(begun + 1 + at)
            pair(head, jnp.maximum(here, there), jnp.minimum(here, there), False)
            return inner

        lax.fori_loop(0, planes - 1 - step, far, 0)

        @pl.when(rising)
        def _():
            hand_keys(head, here)

        @pl.when(jnp.logical_not(rising))
        def _():
            hand_queries(head, here)

        return carry

    lax.fori_loop(0, heads * planes, stage, 0)
    mem_end()
    for load in loads[14:]:
        load.wait()

    def gathered(peer):
        for head in range(heads):
            q_copy(head, peer, peer).wait_recv()
            kv_copy(head, peer, peer).wait_recv()

    half = width // 2

    def gather_plane(step, carry):
        which = lax.rem(my_plane + step, planes)
        for part in range(2):
            peer = 2 * which + part

            @pl.when(peer != me)
            def _():
                gathered(peer)

        columns = rows_of(which, 2 * group)
        for part in range(2):
            here = slice(part * half, (part + 1) * half)
            value = product[here, :]
            for kind in range(3):
                grads = g_recv[kind, pl.ds(2 * which, 2)].reshape(2 * group, length)
                value = value + dot_nn(weights[kind, here, columns], grads)
            product[here, :] = value
        return carry

    lax.fori_loop(0, planes, gather_plane, 0)
    sum_end()
    tile = 256
    for index in range(width // tile):
        here = slice(index * tile, (index + 1) * tile)
        tg_ref[:, here] = (base_ref[:, here] + product[here, :].T).astype(low)
    for other in range(n):

        @pl.when(other != me)
        def _():
            pre_b(other, other).wait_recv()

        value = pre_recv[other].astype(f32)
        for which in range(2):
            pkv_ref[:, which * width + other * group : which * width + (other + 1) * group] = (
                jnp.concatenate(
                    [value[head, :, which * HD : (which + 1) * HD] for head in range(heads)], axis=1
                )
            )

    def drain(peer):
        do_copy(heads - 1, peer, me).wait_send()
        pre_b(peer, me).wait_send()
        for head in range(heads):
            q_copy(head, peer, me).wait_send()
            kv_copy(head, peer, me).wait_send()

    others(n, me, drain)
    others(batches, my_batch, lambda peer: pre_a(peer, my_batch).wait_send())
    others(batches, my_batch, lambda peer: vec_a(peer, my_batch).wait_send())
    reduce_core().wait_send()
    others(highs, my_high, lambda peer: reduce_x(peer, my_high).wait_send())
    reduce_y().wait_send()
    others(planes, my_plane, lambda peer: reduce_z(peer, my_plane).wait_send())
    others(planes, my_plane, lambda peer: gather_z(peer, my_plane).wait_send())
    gather_y(my_side).wait_send()
    others(highs, my_high, lambda peer: gather_x(peer, my_high).wait_send())
    gather_core(my_core).wait_send()
    mem_across().wait_send()
    mem_drain()
    others(planes, my_plane, lambda peer: vec_c(peer, my_plane).wait_send())
    vec_b(my_side).wait_send()
    save_full.wait()


def self_backward(
    n, batches, first_grad, out_grad, sums, mem_grads, mem_weights, vecs, saved, weights
):
    length, width = first_grad.shape
    group = width // n
    heads = group // HD
    whole = n * length
    planes = n // 2
    low = jnp.bfloat16
    f32 = jnp.float32
    vmem = pl.BlockSpec(memory_space=pltpu.VMEM)
    anywhere = pl.BlockSpec(memory_space=pl.ANY)
    dma = pltpu.SemaphoreType.DMA
    sum_rows = sums.shape[0] // (n * batches)
    mem_len = mem_grads[0].shape[0]
    mem_rows = mem_len // n
    mem_part = pltpu.VMEM((planes, mem_rows, width), low)
    mem_low = pltpu.VMEM((mem_len, width), low)
    square = pltpu.VMEM((width, width), low)
    vec = pltpu.VMEM((8, width), f32)
    copies = 6 + 2 * (batches // 2) + 5 * planes + 2 * batches + n
    qx, kx, raw, pk, pv, pkt, ot, stat = (pltpu.VMEM(value.shape, value.dtype) for value in saved)
    return pl.pallas_call(
        functools.partial(self_backward_kernel, n, batches),
        out_shape=(
            jax.ShapeDtypeStruct((length, width), low),
            jax.ShapeDtypeStruct((mem_rows, width), low),
            jax.ShapeDtypeStruct((PREFIX_ROWS, 2 * width), f32),
            jax.ShapeDtypeStruct((8, width), f32),
            jax.ShapeDtypeStruct((2, batches // 2, 2, planes, sum_rows, LANES), low),
        ),
        in_specs=[anywhere] * 19,
        out_specs=(vmem, vmem, vmem, vmem, anywhere),
        scratch_shapes=[
            pltpu.VMEM((heads, n, HD, length), low),
            qx,
            kx,
            raw,
            pltpu.VMEM((heads, HD, whole), low),
            pltpu.VMEM((heads, whole, HD), low),
            pltpu.VMEM((heads, HD, whole), low),
            pltpu.VMEM((heads, whole, 2 * HD), low),
            pk,
            pv,
            pkt,
            ot,
            stat,
            pltpu.VMEM((3, width, width), low),
            pltpu.VMEM((planes, heads, HD, 2 * length), f32),
            pltpu.VMEM((heads, whole, 2 * HD), f32),
            pltpu.VMEM((n, heads, 3, HD, length), low),
            pltpu.VMEM((3, n, heads, HD, length), low),
            pltpu.VMEM((heads, PREFIX_ROWS, 2 * HD), f32),
            pltpu.VMEM((batches, heads, PREFIX_ROWS, 2 * HD), f32),
            pltpu.VMEM((heads, PREFIX_ROWS, 2 * HD), low),
            pltpu.VMEM((n, heads, PREFIX_ROWS, 2 * HD), low),
            pltpu.VMEM((sums.shape[0] // 2, LANES), low),
            pltpu.VMEM((sums.shape[0] // 2, LANES), low),
            pltpu.VMEM((batches // 2, sums.shape[0] // batches, LANES), low),
            pltpu.VMEM((planes * sum_rows, LANES), low),
            pltpu.VMEM((planes, sum_rows, LANES), low),
            pltpu.VMEM((2, batches // 2, 2, planes, sum_rows, LANES), low),
            mem_low,
            mem_low,
            square,
            square,
            pltpu.VMEM((planes, 2, mem_rows, width), low),
            mem_part,
            mem_part,
            mem_part,
            pltpu.VMEM((batches, 8, width), f32),
            vec,
            pltpu.VMEM((2, 8, width), f32),
            pltpu.VMEM((16, width // 2), low),
            pltpu.VMEM((planes, 16, width // 2), low),
            pltpu.VMEM((width, length), f32),
            pltpu.VMEM((length, width), f32),
            dma((heads, n)),
            dma((heads, n)),
            dma((2, heads, n)),
            dma((2, heads, n)),
            dma((19,)),
            dma((copies,)),
            dma((copies,)),
        ],
        compiler_params=pltpu.CompilerParams(
            collective_id=1, has_side_effects=True, vmem_limit_bytes=VMEM_BYTES
        ),
        name="self_backward",
    )(
        first_grad,
        out_grad,
        sums.reshape(2, -1, LANES),
        *mem_grads,
        *mem_weights,
        vecs,
        *saved,
        *weights,
    )


def both_parts(value):
    high = value.astype(jnp.bfloat16).astype(jnp.float32)
    return jnp.concatenate([high, value - high], axis=0).astype(jnp.bfloat16)


def finish_kernel(
    full_in,
    vecs_ref,
    pkv_ref,
    emb_ref,
    first_in,
    fbias_ref,
    second_in,
    token_in,
    mem_in,
    embed_out,
    first_out,
    fbias_out,
    second_out,
    sbias_out,
    down_out,
    dbias_out,
    raise_out,
    rbias_out,
    gain_out,
    shift_out,
    token_out,
    mem_out,
    full_ref,
    first_ref,
    second_ref,
    token_ref,
    mem_ref,
    first_grad,
    second_grad,
    down_grad,
    raise_grad,
    emb,
    hidden,
    out_sem,
    in_sem,
):
    f32 = jnp.float32
    low = jnp.bfloat16
    width = emb_ref.shape[1]
    down = dbias_out.shape[1]
    count = emb_ref.shape[0]
    first = down * width // LANES
    loads = [
        pltpu.make_async_copy(source, target, in_sem.at[index])
        for index, (source, target) in enumerate(
            (
                (full_in.at[first:], full_ref.at[first:]),
                (full_in.at[:first], full_ref.at[:first]),
                (first_in, first_ref),
                (second_in, second_ref),
                (token_in, token_ref),
                (mem_in, mem_ref),
            )
        )
    ]
    for load in loads:
        load.start()
    saves = []

    def save(source, target, rows=None):
        if rows is not None:
            source, target = source.at[rows], target.at[rows]
        copy = pltpu.make_async_copy(source, target, out_sem.at[len(saves)])
        copy.start()
        saves.append(copy)

    loads[0].wait()
    for index in range(width // LANES):
        raise_grad[:, index * LANES : (index + 1) * LANES] = full_ref[
            first + index * down : first + (index + 1) * down, :
        ].astype(f32)
    save(raise_grad, raise_out)
    loads[1].wait()
    for index in range(down // LANES):
        down_grad[:, index * LANES : (index + 1) * LANES] = full_ref[
            index * width : (index + 1) * width, :
        ].astype(f32)
    save(down_grad, down_out)
    for load in loads[4:]:
        load.wait()
    save(token_ref, token_out)
    save(mem_ref, mem_out)
    loads[2].wait()
    emb[...] = jnp.zeros_like(emb)
    emb[:count, :] = emb_ref[...].astype(f32)
    emb_low = emb[...].astype(low)
    row = lax.broadcasted_iota(jnp.int32, hidden.shape, 0)
    hidden[...] = jnp.where(
        row < count, jnp.tanh(dot_nn(emb_low, first_ref[...]) + fbias_ref[...]), 0.0
    )
    value = hidden[...]
    prefix = pkv_ref[...]
    parts = both_parts(prefix)
    hidden_twice = jnp.concatenate([value, value], axis=0).T.astype(low)
    tile = 128
    for index in range(second_grad.shape[0] // tile):
        here = slice(index * tile, (index + 1) * tile)
        second_grad[here, :] = dot_nn(hidden_twice[here, :], parts)
        save(second_grad, second_out, here)
    sbias_out[...] = jnp.sum(prefix, axis=0, keepdims=True)
    loads[3].wait()
    grad = dot_nt(parts, second_ref[...])
    grad = (grad[:PREFIX_ROWS] + grad[PREFIX_ROWS:]) * (1.0 - value * value)
    fbias_out[...] = jnp.sum(grad, axis=0, keepdims=True)
    parts = both_parts(grad)
    emb_twice = jnp.concatenate([emb[...], emb[...]], axis=0).T.astype(low)
    first_grad[...] = dot_nn(emb_twice, parts)
    save(first_grad, first_out)
    back = dot_nt(parts, first_ref[...])
    embed_out[...] = (back[:PREFIX_ROWS] + back[PREFIX_ROWS:])[:count, :]
    rbias_out[...] = vecs_ref[0:1, :]
    dbias_out[...] = vecs_ref[1:2, :down]
    gain_out[...] = vecs_ref[2:5, :]
    shift_out[...] = vecs_ref[5:8, :]
    for copy in saves:
        copy.wait()


def finish(full, vecs, prefix_grad, embed, first, first_bias, second, down, token_grad, memory_grad):
    f32 = jnp.float32
    count, width = embed.shape
    hidden = first.shape[1]
    vmem = pl.BlockSpec(memory_space=pltpu.VMEM)
    anywhere = pl.BlockSpec(memory_space=pl.ANY)
    shapes = (
        (count, width),
        (width, hidden),
        (1, hidden),
        (hidden, 2 * width),
        (1, 2 * width),
        (width, down),
        (1, down),
        (down, width),
        (1, width),
        (3, width),
        (3, width),
    )
    return pl.pallas_call(
        finish_kernel,
        out_shape=tuple(jax.ShapeDtypeStruct(shape, f32) for shape in shapes)
        + tuple(
            jax.ShapeDtypeStruct(value.shape, value.dtype) for value in (token_grad, memory_grad)
        ),
        in_specs=[anywhere, vmem, vmem, vmem, anywhere, vmem, anywhere, anywhere, anywhere],
        out_specs=(
            vmem,
            anywhere,
            vmem,
            anywhere,
            vmem,
            anywhere,
            vmem,
            anywhere,
            vmem,
            vmem,
            vmem,
            anywhere,
            anywhere,
        ),
        scratch_shapes=[
            pltpu.VMEM(full.shape, jnp.bfloat16),
            pltpu.VMEM(first.shape, jnp.bfloat16),
            pltpu.VMEM(second.shape, jnp.bfloat16),
            pltpu.VMEM(token_grad.shape, token_grad.dtype),
            pltpu.VMEM(memory_grad.shape, memory_grad.dtype),
            pltpu.VMEM((width, hidden), f32),
            pltpu.VMEM((hidden, 2 * width), f32),
            pltpu.VMEM((width, down), f32),
            pltpu.VMEM((down, width), f32),
            pltpu.VMEM((PREFIX_ROWS, width), f32),
            pltpu.VMEM((PREFIX_ROWS, hidden), f32),
            pltpu.SemaphoreType.DMA((5 + hidden // 128,)),
            pltpu.SemaphoreType.DMA((6,)),
        ],
        compiler_params=pltpu.CompilerParams(vmem_limit_bytes=VMEM_BYTES),
        name="finish",
    )(full, vecs, prefix_grad, embed, first, first_bias, second, token_grad, memory_grad)


def gelu_pair(value):
    size = jnp.abs(value)
    step = 1.0 / (1.0 + (0.3275911 * 0.7071067811865476) * size)
    bell = jnp.exp(-0.5 * value * value)
    poly = step * (
        0.127414796
        + step
        * (-0.142248368 + step * (0.7107068705 + step * (-0.7265760135 + step * 0.5307027145)))
    )
    act = jnp.maximum(value, 0.0) - size * (poly * bell)
    turn = bell * (0.3989422804014327 * size - poly)
    return act, jnp.where(value >= 0.0, 1.0 + turn, -turn)


def normed(value):
    center = jnp.mean(value, axis=-1, keepdims=True)
    centered = value - center
    scale = lax.rsqrt(jnp.mean(centered * centered, axis=-1, keepdims=True) + norm_eps)
    return centered * scale, scale


def norm_back(grad, scale, unit):
    return scale * (
        grad
        - jnp.mean(grad, axis=-1, keepdims=True)
        - unit * jnp.mean(grad * unit, axis=-1, keepdims=True)
    )


def middle_kernel(
    tok_in,
    att_in,
    cot_in,
    mkey_in,
    mvalue_in,
    gain_ref,
    shift_ref,
    dbias_ref,
    rbias_ref,
    wo_in,
    wcq_in,
    wco_in,
    wd_in,
    wr_in,
    win_in,
    wout_in,
    layer_out,
    fgrad_out,
    ograd_out,
    mkey_out,
    mvalue_out,
    sums_out,
    vecs_ref,
    tok_ref,
    att_ref,
    cot_ref,
    mkey_ref,
    mvalue_ref,
    out_ref,
    fgrad_ref,
    ograd_ref,
    sums_ref,
    wo,
    wcq,
    wco,
    wd,
    wr,
    win,
    wout,
    unit_one,
    unit_two,
    work,
    total,
    scale_one,
    scale_two,
    low_one,
    low_two,
    low_three,
    query,
    crossed,
    weights,
    slopes,
    acts,
    down_act,
    down_slope,
    down_grad,
    load_sem,
    win_sem,
    wout_sem,
    out_sem,
):
    length, width = tok_ref.shape
    resident = len(win.shape) == 2
    tile = 512 if resident else win.shape[2]
    tiles = win_in.shape[1] // tile
    slots = tiles if resident else win.shape[0]
    rows_step = 64
    low = jnp.bfloat16
    f32 = jnp.float32

    sources = (
        att_in,
        wo_in,
        tok_in,
        wcq_in,
        mkey_in,
        mvalue_in,
        wco_in,
        wd_in,
        wr_in,
        cot_in,
    )
    targets = (att_ref, wo, tok_ref, wcq, mkey_ref, mvalue_ref, wco, wd, wr, cot_ref)
    loads = [
        pltpu.make_async_copy(source, target, load_sem.at[index])
        for index, (source, target) in enumerate(zip(sources, targets))
    ]

    def win_load(which):
        slot = which % slots
        target = win.at[:, rows_of(which, tile)] if resident else win.at[slot]
        return pltpu.make_async_copy(win_in.at[:, rows_of(which, tile)], target, win_sem.at[slot])

    def wout_load(which):
        slot = which % slots
        target = wout.at[rows_of(which, tile), :] if resident else wout.at[slot]
        return pltpu.make_async_copy(wout_in.at[rows_of(which, tile), :], target, wout_sem.at[slot])

    for load in loads[:7]:
        load.start()

    def by_columns(extent, step, body):
        def one(index, carry):
            body(pl.ds(pl.multiple_of(index * step, step), step))
            return carry

        lax.fori_loop(0, extent // step, one, 0)

    def by_rows(body, init=0):
        def one(index, carry):
            return body(rows_of(index, rows_step), carry)

        return lax.fori_loop(0, length // rows_step, one, init)

    cols = 512
    half = width // 2

    for load in loads[:3]:
        load.wait()
    for load in loads[7:]:
        load.start()
    for which in range(slots):
        win_load(which).start()
    for which in range(slots):
        wout_load(which).start()

    def project_out(here):
        work[:, here] = tok_ref[:, here].astype(f32) + dot_nn(att_ref[...], wo[:, here])

    by_columns(width, cols, project_out)

    def first_norm(here, carry):
        unit, scale = normed(work[here, :])
        unit_one[here, :] = unit
        scale_one[here, :] = scale
        value = unit * gain_ref[0:1, :] + shift_ref[0:1, :]
        work[here, :] = value
        low_one[here, :] = value.astype(low)
        return carry

    by_rows(first_norm)

    loads[3].wait()

    def project_query(here):
        query[:, here] = dot_nn(low_one[...], wcq[:, here]).astype(low)

    by_columns(width, cols, project_query)
    per_block = LANES // HD

    def stacked(value):
        return jnp.concatenate(
            [jnp.where(head_lanes(value.shape, head), value, 0.0) for head in range(per_block)],
            axis=0,
        ).astype(low)

    def unstacked(value):
        return jnp.concatenate(
            [
                value[head * HD : (head + 1) * HD, head * length : (head + 1) * length]
                for head in range(per_block)
            ],
            axis=0,
        )

    def block_queries(here):
        return stacked(query[:, here].astype(f32) * 0.125)

    def cross_forward(block):
        here = rows_of(block, LANES)
        scores = dot_nt(mkey_ref[:, here], block_queries(here))
        raised = jnp.exp(scores - jnp.max(scores, axis=0, keepdims=True))
        share = 1.0 / jnp.sum(raised, axis=0, keepdims=True)
        weight = (raised * share).astype(low)
        weights[block] = weight
        values = mvalue_ref[:, here].astype(f32).T.astype(low)
        crossed[:, here] = unstacked(dot_nn(values, weight)).T.astype(low)

    loads[4].wait()
    loads[5].wait()

    def cross_forward_both(step, carry):
        cross_forward(2 * step)
        cross_forward(2 * step + 1)
        return carry

    lax.fori_loop(0, width // LANES // 2, cross_forward_both, 0)

    loads[6].wait()

    def project_crossed(here):
        work[:, here] += dot_nn(crossed[...], wco[:, here])

    by_columns(width, cols, project_crossed)

    def second_norm(here, carry):
        unit, scale = normed(work[here, :])
        unit_two[here, :] = unit
        scale_two[here, :] = scale
        value = unit * gain_ref[1:2, :] + shift_ref[1:2, :]
        work[here, :] = value
        low_two[here, :] = value.astype(low)
        return carry

    by_rows(second_norm)

    step_cols = 512

    def feed_part(here, source):
        act, slope = gelu_pair(dot_nn(low_two[...], source))
        slopes[:, here] = slope.astype(low)
        return act.astype(low)

    if resident:

        def feed_forward(which, carry):
            here = rows_of(which, step_cols)

            @pl.when(which % (tile // step_cols) == 0)
            def _():
                win_load(which // (tile // step_cols)).wait()

            acts[:, here] = feed_part(here, win[:, here])
            return carry

        lax.fori_loop(0, tiles * tile // step_cols, feed_forward, 0)
        for which in range(tiles):
            wout_load(which).wait()

        def feed_out_part(here):
            total[:, here] = dot_nn(acts[...], wout[:, here])

        by_columns(width, step_cols, feed_out_part)
    else:
        total[...] = jnp.zeros_like(total)

        def feed_forward(which, carry):
            slot = lax.rem(which, slots)
            win_load(which).wait()
            wout_load(which).wait()
            total[...] += dot_nn(feed_part(rows_of(which, tile), win[slot]), wout[slot])

            @pl.when(which + slots < tiles)
            def _():
                win_load(which + slots).start()
                wout_load(which + slots).start()

            return carry

        lax.fori_loop(0, tiles, feed_forward, 0)

    loads[7].wait()
    loads[8].wait()
    loads[9].wait()
    act, slope = gelu_pair(dot_nn(low_two[...], wd[...]) + dbias_ref[...])
    down_act[...] = act.astype(low)
    down_slope[...] = slope.astype(low)

    def project_raise(here):
        work[:, here] += total[:, here] + 4.0 * (
            dot_nn(down_act[...], wr[:, here]) + rbias_ref[:, here]
        )

    by_columns(width, cols, project_raise)
    nothing = jnp.zeros((1, width), f32)

    def third_norm(here, carry):
        gain_sum, shift_sum, bias_sum = carry
        unit, scale = normed(work[here, :])
        gain = gain_ref[2:3, :]
        out_ref[here, :] = (unit * gain + shift_ref[2:3, :]).astype(low)
        grad = cot_ref[here, :].astype(f32)
        back = norm_back(grad * gain, scale, unit)
        total[here, :] = back
        back_low = back.astype(low)
        low_three[here, :] = back_low
        return (
            gain_sum + jnp.sum(grad * unit, axis=0, keepdims=True),
            shift_sum + jnp.sum(grad, axis=0, keepdims=True),
            bias_sum + jnp.sum(back_low.astype(f32), axis=0, keepdims=True),
        )

    gain_three, shift_three, bias_sum = by_rows(third_norm, (nothing, nothing, nothing))
    saves = []

    def save(source, target):
        copy = pltpu.make_async_copy(source, target, out_sem.at[len(saves)])
        copy.start()
        saves.append(copy)

    save(out_ref, layer_out)
    vecs_ref[0:1, :] = 4.0 * bias_sum

    back = 4.0 * dot_nt(low_three[...], wr[...]) * down_slope[...].astype(f32)
    back_low = back.astype(low)
    down_grad[...] = back_low
    vecs_ref[1:2, :] = jnp.concatenate(
        [
            jnp.sum(back_low.astype(f32), axis=0, keepdims=True),
            jnp.zeros((1, width - wd.shape[1]), f32),
        ],
        axis=1,
    )
    down = wd.shape[1]
    raise_sum = 4.0 * dot_tn(down_act[...], low_three[...])
    for index in range(width // LANES):
        sums_ref[pl.ds(down * width // LANES + index * down, down), :] = raise_sum[
            :, index * LANES : (index + 1) * LANES
        ].astype(low)
    down_sum = dot_tn(low_two[...], down_grad[...])
    for index in range(down // LANES):
        sums_ref[index * width : (index + 1) * width, :] = down_sum[
            :, index * LANES : (index + 1) * LANES
        ].astype(low)

    save(sums_ref, sums_out)

    if resident:

        def feed_slope(here):
            acts[:, here] = (
                dot_nt(low_three[...], wout[here, :]) * slopes[:, here].astype(f32)
            ).astype(low)

        by_columns(win_in.shape[1], step_cols, feed_slope)

        def feed_in_part(here):
            total[:, here] += dot_nt(acts[...], win[here, :])

        by_columns(width, step_cols, feed_in_part)
    else:

        def feed_backward(step, carry):
            which = tiles - 1 - step
            slot = lax.rem(which, slots)
            here = rows_of(which, tile)

            @pl.when(which < tiles - slots)
            def _():
                wout_load(which).wait()
                win_load(which).wait()

            grad = dot_nt(low_three[...], wout[slot]) * slopes[:, here].astype(f32)
            total[...] += dot_nt(grad.astype(low), win[slot])

            @pl.when(which >= slots)
            def _():
                win_load(which - slots).start()
                wout_load(which - slots).start()

            return carry

        lax.fori_loop(0, tiles, feed_backward, 0)

    def down_back(here):
        total[:, here] += dot_nt(down_grad[...], wd[here, :])

    by_columns(width, cols, down_back)

    def second_back(here, carry):
        gain_sum, shift_sum = carry
        grad = total[here, :]
        unit = unit_two[here, :]
        back = norm_back(grad * gain_ref[1:2, :], scale_two[here, :], unit)
        total[here, :] = back
        low_one[here, :] = back.astype(low)
        return (
            gain_sum + jnp.sum(grad * unit, axis=0, keepdims=True),
            shift_sum + jnp.sum(grad, axis=0, keepdims=True),
        )

    gain_two, shift_two = by_rows(second_back, (nothing, nothing))

    def crossed_back(here):
        crossed[:, here] = dot_nt(low_one[...], wco[here, :]).astype(low)

    by_columns(width, cols, crossed_back)

    def cross_backward(block):
        here = rows_of(block, LANES)
        grads = stacked(crossed[:, here].astype(f32))
        keys = mkey_ref[:, here].astype(f32).T.astype(low)
        slope = dot_nt(mvalue_ref[:, here], grads)
        weight_low = weights[block]
        weight = weight_low.astype(f32)
        slope = weight * (slope - jnp.sum(weight * slope, axis=0, keepdims=True))
        slope = slope.astype(low)
        queries = block_queries(here)
        mkey_ref[:, here] = dot_nn(slope, queries).astype(low)
        mvalue_ref[:, here] = dot_nn(weight_low, grads).astype(low)
        query[:, here] = (unstacked(dot_nn(keys, slope)) * 0.125).T.astype(low)

    def cross_backward_both(step, carry):
        cross_backward(2 * step)
        cross_backward(2 * step + 1)
        return carry

    lax.fori_loop(0, width // LANES // 2, cross_backward_both, 0)
    save(mkey_ref, mkey_out)
    save(mvalue_ref, mvalue_out)

    def query_back(here):
        total[:, here] += dot_nt(query[...], wcq[here, :])

    by_columns(width, cols, query_back)

    def first_back(here, carry):
        gain_sum, shift_sum = carry
        grad = total[here, :]
        unit = unit_one[here, :]
        back = norm_back(grad * gain_ref[0:1, :], scale_one[here, :], unit)
        fgrad_ref[here, :] = back
        low_one[here, :] = back.astype(low)
        return (
            gain_sum + jnp.sum(grad * unit, axis=0, keepdims=True),
            shift_sum + jnp.sum(grad, axis=0, keepdims=True),
        )

    gain_one, shift_one = by_rows(first_back, (nothing, nothing))
    save(fgrad_ref, fgrad_out)

    for index in range(width // cols):
        here = slice(index * cols, (index + 1) * cols)
        ograd_ref[here, :] = dot_nt(low_one[...], wo[here, :]).T.astype(low)
        save(ograd_ref.at[here], ograd_out.at[here])
    for index, vector in enumerate(
        (gain_one, gain_two, gain_three, shift_one, shift_two, shift_three)
    ):
        vecs_ref[2 + index : 3 + index, :] = vector
    for copy in saves:
        copy.wait()


def middle(
    tokens, attended, cotangent, mem_key, mem_value, gains, shifts, down_bias, raise_bias, weights
):
    length, width = tokens.shape
    mem_len = mem_key.shape[0]
    down = weights[3].shape[1]
    feed = weights[5].shape[1]
    tile = 512 if mem_len <= 512 else 128
    resident = mem_len <= 512
    slots = feed // tile if resident else 2
    low = jnp.bfloat16
    f32 = jnp.float32
    vmem = pl.BlockSpec(memory_space=pltpu.VMEM)
    anywhere = pl.BlockSpec(memory_space=pl.ANY)
    square = pltpu.VMEM((width, width), low)
    wide = pltpu.VMEM((length, width), f32)
    narrow = pltpu.VMEM((length, width), low)
    return pl.pallas_call(
        middle_kernel,
        out_shape=(
            jax.ShapeDtypeStruct((length, width), low),
            jax.ShapeDtypeStruct((length, width), f32),
            jax.ShapeDtypeStruct((width, length), low),
            jax.ShapeDtypeStruct((mem_len, width), low),
            jax.ShapeDtypeStruct((mem_len, width), low),
            jax.ShapeDtypeStruct((2 * down * width // LANES, LANES), low),
            jax.ShapeDtypeStruct((8, width), f32),
        ),
        in_specs=[anywhere] * 5 + [vmem] * 4 + [anywhere] * 7,
        out_specs=(anywhere,) * 6 + (vmem,),
        scratch_shapes=[
            narrow,
            narrow,
            narrow,
            pltpu.VMEM((mem_len, width), low),
            pltpu.VMEM((mem_len, width), low),
            narrow,
            wide,
            pltpu.VMEM((width, length), low),
            pltpu.VMEM((2 * down * width // LANES, LANES), low),
            square,
            square,
            square,
            pltpu.VMEM((width, down), low),
            pltpu.VMEM((down, width), low),
            pltpu.VMEM((width, feed) if resident else (slots, width, tile), low),
            pltpu.VMEM((feed, width) if resident else (slots, tile, width), low),
            wide,
            wide,
            wide,
            wide,
            pltpu.VMEM((length, 1), f32),
            pltpu.VMEM((length, 1), f32),
            narrow,
            narrow,
            narrow,
            narrow,
            narrow,
            pltpu.VMEM((width // LANES, mem_len, LANES // HD * length), low),
            pltpu.VMEM((length, feed), low),
            pltpu.VMEM((length, feed) if resident else (16, LANES), low),
            pltpu.VMEM((length, down), low),
            pltpu.VMEM((length, down), low),
            pltpu.VMEM((length, down), low),
            pltpu.SemaphoreType.DMA((10,)),
            pltpu.SemaphoreType.DMA((slots,)),
            pltpu.SemaphoreType.DMA((slots,)),
            pltpu.SemaphoreType.DMA((5 + width // 512,)),
        ],
        compiler_params=pltpu.CompilerParams(vmem_limit_bytes=VMEM_BYTES + 3 * 1024 * 1024),
        name="middle",
    )(tokens, attended, cotangent, mem_key, mem_value, gains, shifts, down_bias, raise_bias, *weights)


def per_device(
    tokens,
    memory,
    segment_ids,
    padding_mask,
    cotangent,
    prefix_embed,
    prefix_first,
    first_bias,
    prefix_second,
    second_bias,
    adapter_down,
    down_bias,
    adapter_raise,
    raise_bias,
    norm_gain,
    norm_shift,
    self_query,
    self_key,
    self_value,
    self_output,
    cross_query,
    cross_key,
    cross_value,
    cross_output,
    feed_in,
    feed_out,
):
    row_count, length, model_width = tokens.shape
    flat_rows = row_count * length
    n = lax.axis_size("seq")
    batches = lax.axis_size("batch")
    down = adapter_down.shape[1]
    attended, mem_key, mem_value, *saved = self_forward(
        n,
        segment_ids,
        padding_mask,
        tokens.reshape(flat_rows, model_width),
        (self_query, self_key, self_value),
        (
            prefix_embed,
            prefix_first,
            first_bias.reshape(1, -1),
            prefix_second,
            second_bias.reshape(1, -1),
        ),
        memory.reshape(-1, model_width),
        (cross_key, cross_value),
    )
    layer_output, first_grad, out_grad, *mem_grads, weight_sums, vector_sums = middle(
        tokens.reshape(flat_rows, model_width),
        attended,
        cotangent.reshape(flat_rows, model_width),
        mem_key,
        mem_value,
        norm_gain,
        norm_shift,
        down_bias.reshape(1, -1),
        raise_bias.reshape(1, -1),
        (
            self_output,
            cross_query,
            cross_output,
            adapter_down,
            adapter_raise,
            feed_in,
            feed_out,
        ),
    )
    layer_output = layer_output.reshape(row_count, length, model_width)
    token_grad, memory_grad, prefix_grad, vector_sums, full_sums = self_backward(
        n,
        batches,
        first_grad,
        out_grad.reshape(n, -1, HD, length),
        weight_sums,
        mem_grads,
        (cross_key, cross_value),
        vector_sums,
        saved,
        (self_query, self_key, self_value),
    )
    *replicated, token_grad, memory_grad = finish(
        full_sums.reshape(-1, LANES),
        vector_sums,
        prefix_grad,
        prefix_embed,
        prefix_first,
        first_bias.reshape(1, -1),
        prefix_second,
        down,
        token_grad,
        memory_grad,
    )
    token_grad = token_grad.reshape(row_count, length, model_width)
    memory_grad = memory_grad.reshape(memory.shape)
    replicated = [
        value.reshape(-1) if value.shape[0] == 1 else value for value in replicated
    ]
    return (layer_output, token_grad, memory_grad, *replicated)


def solution(mesh):
    placed = (
        P("batch", "seq", None),
        P("batch", "seq", None),
        P("batch", "seq"),
        P("batch", "seq"),
        P("batch", "seq", None),
        P(),
        P(),
        P(),
        P(),
        P(),
        P(),
        P(),
        P(),
        P(),
        P(),
        P(),
        P(),
        P(),
        P(),
        P(),
        P(),
        P(),
        P(),
        P(),
        P(),
        P(),
    )
    return jax.shard_map(
        per_device,
        mesh=mesh,
        in_specs=placed,
        out_specs=(
            P("batch", "seq", None),
            P("batch", "seq", None),
            P("batch", "seq", None),
            P(),
            P(),
            P(),
            P(),
            P(),
            P(),
            P(),
            P(),
            P(),
            P(),
            P(),
        ),
        check_vma=False,
    )
```

profile of v0, /device:TPU:0, one launch (start us, length us, event | category | flops | bytes accessed | tf_op | source)
XLA Modules:
  0.0 273.1 jit_solution(17655473149605888233)
XLA Ops:
  0.6 93.4 %self_forward.1 = (bf16[384,1024]{1,0:T(8,128)(2,1)}, bf16[512,1024]{1,0:T(8,128)(2,1)}, bf16[512,1024]{1,0:T(8,128)(2,1)}, bf16[2,128,3072]{2,1,0:T(8,128)(2,1)...) custom-call(s32[1,384]{1,0:T(1,128)} %seg_ref.1, ...), custom_call_target="tpu_custom_call" | custom-call | tf_op jit(solution)/shard_map/self_forward/pallas_call | solution.py:543
  94.1 60.8 %middle.1 = (bf16[384,1024]{1,0:T(8,128)(2,1)}, f32[384,1024]{1,0:T(8,128)}, bf16[1024,384]{1,0:T(8,128)(2,1)}, bf16[512,1024]{1,0:T(8,128)(2,1)}, bf16[512,1024...) custom-call(bf16[384,1024]{1,0:T(8,128)(2,1)} %bitcast.18, ...), custom_call_target="tpu_custom_call" | custom-call | tf_op jit(solution)/shard_map/middle/pallas_call | solution.py:2062
  154.9 109.1 %self_backward.1 = (bf16[384,1024]{1,0:T(8,128)(2,1)}, bf16[64,1024]{1,0:T(8,128)(2,1)}, f32[32,2048]{1,0:T(8,128)}, f32[8,1024]{1,0:T(8,128)}, bf16[2,2,2,4,256,128]{5,4,3,2,1,0:T(8,128)(2,1)}) custom-call(f32[384,1024]{1,0:T(8,128)} %get-tuple-element.54.base_in, bf16[8,2,64,384]{3,2,1,0:T(8,128)(2,1)} %bitcast.21, bf16[2,4096,128]{2,1,0:T(8,128)(2,1)} %bitcast.19, ...), custom_call_target="tpu_custom_call" | custom-call | tf_op jit(solution)/shard_map/self_backward/pallas_call | solution.py:1318
  264.0 8.9 %finish.1 = (f32[30,1024]{1,0:T(8,128)}, f32[1024,512]{1,0:T(8,128)}, f32[1,512]{1,0:T(1,128)}, f32[512,2048]{1,0:T(8,128)}, f32[1,2048]{1,0:T(1,128)}, /*index=...) custom-call(bf16[8192,128]{1,0:T(8,128)(2,1)} %bitcast.20, ...), custom_call_target="tpu_custom_call" | custom-call | tf_op jit(solution)/shard_map/finish/pallas_call | solution.py:1540
where the time goes:
time: 273 us
  Pallas kernels  272 us (100%)
    pallas_call x1, Pallas kernels, self_backward(): pl.pallas_call(functools.partial(self_backward_kernel, n, batches), out_s...  109 us
    pallas_call x1, Pallas kernels, self_forward(): pl.pallas_call(functools.partial(self_forward_kernel, n), out_shape=(jax....  93.4 us
    pallas_call x1, Pallas kernels, middle(): pl.pallas_call(middle_kernel, out_shape=(jax.ShapeDtypeStruct((length, wi...  60.8 us
    pallas_call x1, Pallas kernels, finish(): pl.pallas_call(finish_kernel, out_shape=tuple((jax.ShapeDtypeStruct(shape...  8.86 us

commit v1 on v0

--- a/solution.py
+++ b/solution.py
@@ -1082,8 +1082,8 @@
 
     save_full = pltpu.make_async_copy(full, full_out, in_sem.at[0])
 
-    def pair_part(head, upper, lower, first, count, diagonal):
-        keys = span_of(lower * plane + first, count)
+    def pair_part(head, upper, lower, first, count, diagonal, at=None):
+        keys = span_of(lower * plane + (first if at is None else at * count), count)
         here = span_of(upper * plane + first, plane - first)
         at = slice(first, plane)
         scores = dot_nn(kx[head, keys, :], qx[head, :, here])
@@ -1101,10 +1101,15 @@
 
     def pair(head, upper, lower, diagonal):
         if diagonal:
-            pair_part(head, upper, lower, 0, length, True)
-            pair_part(head, upper, lower, length, length, True)
+            for part in range(plane // step_rows):
+                pair_part(head, upper, lower, part * step_rows, step_rows, True)
         else:
-            pair_part(head, upper, lower, 0, plane, False)
+
+            def one(at, carry):
+                pair_part(head, upper, lower, 0, step_rows, False, at)
+                return carry
+
+            lax.fori_loop(0, plane // step_rows, one, 0)
 
     def hand_queries(head, which):
         for part in range(2):
@@ -1675,7 +1680,7 @@
     tile = 512 if resident else win.shape[2]
     tiles = win_in.shape[1] // tile
     slots = tiles if resident else win.shape[0]
-    rows_step = 64
+    rows_step = length // 2
     low = jnp.bfloat16
     f32 = jnp.float32
 

time: 273 us -> 276 us (1.011); the launches traced: 273 us -> 272 us
    pallas_call x1, Pallas kernels: 60.8 us -> 58 us  [middle(): pl.pallas_call(middle_kernel, out_shape=(jax.ShapeDtypeStruct((length, wi...]
where the time goes in v1:
time: 276 us; the launch traced here: 272 us
  Pallas kernels  271 us (98%)
    pallas_call x1, Pallas kernels, self_backward(): pl.pallas_call(functools.partial(self_backward_kernel, n, batches), out_s...  110 us
    pallas_call x1, Pallas kernels, self_forward(): pl.pallas_call(functools.partial(self_forward_kernel, n), out_shape=(jax....  93.4 us
    pallas_call x1, Pallas kernels, middle(): pl.pallas_call(middle_kernel, out_shape=(jax.ShapeDtypeStruct((length, wi...  58 us
    pallas_call x1, Pallas kernels, finish(): pl.pallas_call(finish_kernel, out_shape=tuple((jax.ShapeDtypeStruct(shape...  8.86 us

profile of v1, /device:TPU:0, one launch (start us, length us, event | category | flops | bytes accessed | tf_op | source)
XLA Modules:
  0.0 271.7 jit_solution(13112767474729704460)
XLA Ops:
  0.6 93.4 %self_forward.1 = (bf16[384,1024]{1,0:T(8,128)(2,1)}, bf16[512,1024]{1,0:T(8,128)(2,1)}, bf16[512,1024]{1,0:T(8,128)(2,1)}, bf16[2,128,3072]{2,1,0:T(8,128)(2,1)...) custom-call(s32[1,384]{1,0:T(1,128)} %seg_ref.1, ...), custom_call_target="tpu_custom_call" | custom-call | tf_op jit(solution)/shard_map/self_forward/pallas_call | solution.py:543
  94.1 58.0 %middle.1 = (bf16[384,1024]{1,0:T(8,128)(2,1)}, f32[384,1024]{1,0:T(8,128)}, bf16[1024,384]{1,0:T(8,128)(2,1)}, bf16[512,1024]{1,0:T(8,128)(2,1)}, bf16[512,1024...) custom-call(bf16[384,1024]{1,0:T(8,128)(2,1)} %bitcast.18, ...), custom_call_target="tpu_custom_call" | custom-call | tf_op jit(solution)/shard_map/middle/pallas_call | solution.py:2067
  152.1 110.5 %self_backward.1 = (bf16[384,1024]{1,0:T(8,128)(2,1)}, bf16[64,1024]{1,0:T(8,128)(2,1)}, f32[32,2048]{1,0:T(8,128)}, f32[8,1024]{1,0:T(8,128)}, bf16[2,2,2,4,256,128]{5,4,3,2,1,0:T(8,128)(2,1)}) custom-call(f32[384,1024]{1,0:T(8,128)} %get-tuple-element.54.base_in, bf16[8,2,64,384]{3,2,1,0:T(8,128)(2,1)} %bitcast.21, bf16[2,4096,128]{2,1,0:T(8,128)(2,1)} %bitcast.19, ...), custom_call_target="tpu_custom_call" | custom-call | tf_op jit(solution)/shard_map/self_backward/pallas_call | solution.py:1323
  262.6 8.9 %finish.1 = (f32[30,1024]{1,0:T(8,128)}, f32[1024,512]{1,0:T(8,128)}, f32[1,512]{1,0:T(1,128)}, f32[512,2048]{1,0:T(8,128)}, f32[1,2048]{1,0:T(1,128)}, /*index=...) custom-call(bf16[8192,128]{1,0:T(8,128)(2,1)} %bitcast.20, ...), custom_call_target="tpu_custom_call" | custom-call | tf_op jit(solution)/shard_map/finish/pallas_call | solution.py:1545
